TPU v7x, 1024 devices: a whole 4x8x16 slice. The times are simulated.
1024 devices in a mesh: fsdp: 32 (over x, z_hi, core), ep: 32 (over y, z_lo).
Axes of the slice: x: 4, y: 8, z: 16 (z_hi: 4, z_lo: 4; z = z_hi * 4 + z_lo), core: 2. Of those that a mesh axis runs over, the one named last changes fastest.
Arguments:
- x_resid: bfloat16 [1024, 64, 2048], P(('fsdp', 'ep')), may hold values from -1.5 to 1.5
- q_latent: bfloat16 [1024, 64, 8, 512], P(('fsdp', 'ep')), may hold values from -3 to 3
- q_rope: bfloat16 [1024, 64, 8, 64], P(('fsdp', 'ep')), may hold values from -27 to 27
- cache_latent: bfloat16 [1024, 64, 512], P(('fsdp', 'ep')), may hold values from -6 to 6
- cache_rope: bfloat16 [1024, 64, 64], P(('fsdp', 'ep')), may hold values from -6 to 6
- new_latent: bfloat16 [1024, 64, 512], P(('fsdp', 'ep')), may hold values from -6 to 6
- new_rope: bfloat16 [1024, 64, 64], P(('fsdp', 'ep')), may hold values from -6 to 6
- w_uv: bfloat16 [512, 8, 128], P('fsdp'), may hold values from -0.25 to 0.25
- w_out: bfloat16 [1024, 2048], P('fsdp'), may hold values from -0.1875 to 0.1875
- norm_gain: float32 [2048], replicated, may hold values from 0.5 to 2
- router: bfloat16 [2048, 32], replicated, may hold values from -0.026516504 to 0.026516504
- expert_ids: int32 [1024, 64, 6], P(('fsdp', 'ep')), may hold values from 0 to 31, all different within a row; in each aligned block of 64 rows (0 to 63, 64 to 127, ..., all dimensions but the last counted through in order) at most 12 rows name the same one
- w_gate: bfloat16 [32, 2048, 704], P('ep'), may hold values from -0.125 to 0.125
- w_up: bfloat16 [32, 2048, 704], P('ep'), may hold values from -0.125 to 0.125
- w_down: bfloat16 [32, 704, 2048], P('ep'), may hold values from -0.21875 to 0.21875
Outputs:
- attended: bfloat16 [1024, 64, 2048], P(('fsdp', 'ep'))
- layer_out: bfloat16 [1024, 64, 2048], P(('fsdp', 'ep'))
Inputs may be any that keep to these rules, and one draw needn't show every extreme that they name: `expert_ids`: within the 64 tokens of one sequence every expert is named exactly 12 times.
All inputs are finite; a program needn't handle non-finite values.
Results may differ from a plain program's by a relative error of at most 0.008.
Values may be sent and summed in bfloat16 or wider, within the bound.
A program may use at most 64 MiB of HBM per device.

v0:
```python
import jax
import jax.numpy as jnp
from jax import lax
from jax.sharding import PartitionSpec as P

softmax_scale = 0.07216878364870323
epsilon = 1e-06


def in_order(blocks, dim):
    blocks = jnp.moveaxis(blocks, 0, dim)
    lengths = blocks.shape
    return blocks.reshape(*lengths[:dim], lengths[dim] * lengths[dim + 1], *lengths[dim + 2 :])


def from_everyone(array, axis):
    copies = jnp.broadcast_to(array, (lax.axis_size(axis), *array.shape))
    return lax.all_to_all(copies, axis, split_axis=0, concat_axis=0, tiled=True)


def gather_directly(array, axis, dim):
    return in_order(from_everyone(array, axis), dim)


def attend_local(q_latent, q_rope, cache_latent, cache_rope, new_latent, new_rope):
    new_count, head_count, latent_width = q_latent.shape
    cache_count = cache_latent.shape[0]
    keys_latent = jnp.concatenate([cache_latent, new_latent], 0)
    keys_rope = jnp.concatenate([cache_rope, new_rope], 0)
    query_rows = q_latent.reshape(new_count * head_count, latent_width)
    rope_rows = q_rope.reshape(new_count * head_count, q_rope.shape[2])
    scores = jnp.dot(query_rows, keys_latent.T, preferred_element_type=jnp.float32)
    scores = (
        scores + jnp.dot(rope_rows, keys_rope.T, preferred_element_type=jnp.float32)
    ) * softmax_scale
    token_of_row = jnp.arange(new_count * head_count, dtype=jnp.int32) // head_count
    key_index = jnp.arange(keys_latent.shape[0], dtype=jnp.int32)
    visible = key_index[None, :] <= token_of_row[:, None] + cache_count
    row_top = jnp.max(jnp.where(visible, scores, -jnp.inf), axis=1, keepdims=True)
    exponent = jnp.where(visible, jnp.exp(scores - row_top), 0.0)
    weights_att = (exponent / jnp.sum(exponent, axis=1, keepdims=True)).astype(jnp.bfloat16)
    mixed_latent = jnp.dot(weights_att, keys_latent, preferred_element_type=jnp.float32).astype(
        jnp.bfloat16
    )
    return mixed_latent.reshape(new_count, head_count, latent_width)


def per_device(
    x_resid,
    q_latent,
    q_rope,
    cache_latent,
    cache_rope,
    new_latent,
    new_rope,
    w_uv,
    w_out,
    norm_gain,
    router,
    expert_ids,
    w_gate,
    w_up,
    w_down,
):
    mixed_latent = attend_local(
        q_latent[0], q_rope[0], cache_latent[0], cache_rope[0], new_latent[0], new_rope[0]
    )
    new_count, head_count, latent_width = mixed_latent.shape
    section = mixed_latent
    heads_out = jnp.einsum(
        "thl,lhv->thv",
        section,
        gather_directly(w_uv, "fsdp", 0),
        preferred_element_type=jnp.float32,
    )
    heads_flat = heads_out.astype(jnp.bfloat16).reshape(new_count, -1)
    section = heads_flat
    projected = jnp.dot(
        section,
        lax.all_gather(w_out, "fsdp", axis=0, tiled=True),
        preferred_element_type=jnp.float32,
    )
    hidden = x_resid[0].astype(jnp.float32) + projected
    normed = hidden * lax.rsqrt(jnp.mean(hidden * hidden, axis=-1, keepdims=True) + epsilon)
    normed = (normed * norm_gain).astype(jnp.bfloat16)
    logits = jnp.dot(normed, router, preferred_element_type=jnp.float32)
    expert_count = lax.axis_size("ep")
    top_count = expert_ids.shape[2]
    capacity = new_count * top_count // expert_count
    own_ids = expert_ids[0]
    choose = (own_ids[..., None] == jnp.arange(expert_count, dtype=jnp.int32)).astype(jnp.float32)
    picked = jnp.sum(choose * logits[:, None, :], axis=-1)
    gate_weights = jax.nn.softmax(picked, axis=-1)
    assigned = choose.reshape(-1, expert_count)
    earlier = jnp.cumsum(assigned, axis=0) - assigned
    slot_index = jnp.sum(earlier * assigned, axis=-1).reshape(own_ids.shape).astype(jnp.int32)
    target = own_ids * capacity + slot_index
    placed = jnp.sum(
        (target[..., None] == jnp.arange(expert_count * capacity, dtype=jnp.int32)).astype(
            jnp.bfloat16
        ),
        axis=1,
    )
    buffers = jnp.einsum("tp,td->pd", placed, normed, preferred_element_type=jnp.float32).astype(
        jnp.bfloat16
    )
    buffers = buffers.reshape(expert_count, capacity, -1)
    received = lax.all_to_all(buffers, "ep", split_axis=0, concat_axis=0, tiled=True)
    source_count, slot_count, width = received.shape
    buffer_rows = received.reshape(source_count * slot_count, width)
    gate_proj = jnp.dot(buffer_rows, w_gate[0], preferred_element_type=jnp.float32)
    up_proj = jnp.dot(buffer_rows, w_up[0], preferred_element_type=jnp.float32)
    activated = (jax.nn.silu(gate_proj) * up_proj).astype(jnp.bfloat16)
    result = jnp.dot(activated, w_down[0], preferred_element_type=jnp.float32).astype(jnp.bfloat16)
    result = result.reshape(source_count, slot_count, width)
    returned = lax.all_to_all(result, "ep", split_axis=0, concat_axis=0, tiled=True)
    returned_rows = returned.reshape(expert_count * capacity, -1)[target]
    routed_sum = jnp.sum(gate_weights[..., None] * returned_rows.astype(jnp.float32), axis=1)
    return (hidden.astype(jnp.bfloat16)[None], (hidden + routed_sum).astype(jnp.bfloat16)[None])


def solution(mesh):
    placed = (
        P(("fsdp", "ep"), None, None),
        P(("fsdp", "ep"), None, None, None),
        P(("fsdp", "ep"), None, None, None),
        P(("fsdp", "ep"), None, None),
        P(("fsdp", "ep"), None, None),
        P(("fsdp", "ep"), None, None),
        P(("fsdp", "ep"), None, None),
        P("fsdp", None, None),
        P("fsdp", None),
        P(),
        P(),
        P(("fsdp", "ep"), None, None),
        P("ep", None, None),
        P("ep", None, None),
        P("ep", None, None),
    )
    return jax.shard_map(
        per_device,
        mesh=mesh,
        in_specs=placed,
        out_specs=(P(("fsdp", "ep"), None, None), P(("fsdp", "ep"), None, None)),
        check_vma=False,
    )
```

profile of v0, /device:TPU:6, one launch (start us, length us, event | category | flops | bytes accessed | tf_op | source)
XLA Modules:
  0.0 329.2 jit_solution(18386827265984141482)
XLA Ops:
  7.2 0.0 copy-start
  7.2 0.0 copy-start.4
  7.2 0.0 copy-start.1
  7.2 0.0 all-gather.2.cloned.1.call-start
  7.2 0.7 all-gather.2.cloned.1.call-update
  7.9 0.8 copy.41
  8.8 1.3 broadcast_in_dim.15
  10.0 21.9 %all-to-all-start = ((bf16[32,16,8,128]{3,1,2,0:T(8,128)(2,1)}), bf16[32,16,8,128]{3,1,2,0:T(8,128)(2,1)}, u32[]{:S(2)}, u32[]{:S(2)}) async-start(bf16[32,16,8,128]{3,1,2,0:T(8,128)(2,1)} %broadcast_in_dim.15), calls=%async_computation | async-start | bytes 2097152 | tf_op jit(solution)/shard_map/all_to_all | solution.py:18
  31.9 0.0 copy-done.4
  32.0 0.1 copy.45
  32.1 0.7 eq.51
  32.8 0.1 eq.55
  32.9 0.9 reduce-window.6
  33.8 0.2 slice_reduce_fusion
  34.0 0.8 fusion.38
  34.8 0.1 convert_element_type.82
  35.0 0.1 copy.51
  35.0 0.1 fusion.26
  35.2 0.0 copy-done.1
  35.2 1.2 fusion.23
  36.4 0.0 copy-done.3
  36.4 1.1 select_reduce_fusion
  37.5 0.1 fusion.28
  37.6 1.2 fusion.15
  38.8 40.6 %all-to-all-done = bf16[32,16,8,128]{3,1,2,0:T(8,128)(2,1)} async-done(((bf16[32,16,8,128]{3,1,2,0:T(8,128)(2,1)}), bf16[32,16,8,128]{3,1,2,0:T(8,128)(2,1)}, u32[]{:S(2)}, u32[]{:S(2)}) %all-to-all-start) | async-done | bytes 1048608 | tf_op jit(solution)/shard_map/all_to_all | solution.py:18
  79.4 1.4 copy.42
  80.9 1.0 fusion.18
  81.9 75.7 %all-gather.2.cloned.1.call-done = bf16[1024,2048]{1,0:T(8,128)(2,1)} async-done(((bf16[32,2048]{1,0:T(8,128)(2,1)}), bf16[1024,2048]{1,0:T(8,128)(2,1)}) %all-gather.2.cloned.1.call-update) | async-done | bytes 4194320 | tf_op jit(solution)/shard_map/all_gather | solution.py:80
  157.6 3.2 multiply_reduce_fusion.1
  160.8 0.0 copy-done.2
  160.8 1.8 convolution_convert_fusion
  162.6 3.6 %reshape.154 = bf16[32,12,2048]{2,1,0:T(8,128)(2,1)} reshape(bf16[384,2048]{1,0:T(8,128)(2,1)} %convolution_convert_fusion) | data formatting | bytes 3145728 | tf_op jit(solution)/shard_map/reshape | solution.py:107
  166.2 60.7 %all_to_all.15 = bf16[32,12,2048]{2,1,0:T(8,128)(2,1)} all-to-all(bf16[32,12,2048]{2,1,0:T(8,128)(2,1)} %reshape.154), channel_id=1, replica_groups=mesh['fsdp'=32,'ep'=32] {'ep'}, dimensions={0} | all-to-all | bytes 3145728 | tf_op jit(solution)/shard_map/all_to_all | solution.py:108
  226.9 3.6 %reshape.155 = bf16[384,2048]{1,0:T(8,128)(2,1)} reshape(bf16[32,12,2048]{2,1,0:T(8,128)(2,1)} %all_to_all.15) | data formatting | bytes 3145728 | tf_op jit(solution)/shard_map/reshape | solution.py:110
  230.5 4.9 %fusion.4 = f32[384,704]{0,1:T(8,128)} fusion(bf16[384,2048]{1,0:T(8,128)(2,1)} %reshape.155, bf16[1,2048,704]{1,2,0:T(8,128)(2,1)} %param.27), kind=kOutput, calls=%fused_computation.6 | convolution fusion | flops 1107296256 | bytes 5537792 | tf_op jit(solution)/shard_map/dot_general | solution.py:111
  235.5 6.8 %fusion.6 = bf16[384,2048]{1,0:T(8,128)(2,1)} fusion(bf16[1,704,2048]{2,1,0:T(8,128)(2,1)S(1)} %copy-done, bf16[384,2048]{1,0:T(8,128)(2,1)} %reshape.155, bf16[1,2048,704]{1,2,0:T(8,128)(2,1)} %param.28, f32[384,704]{0,1:T(8,128)} %fusion.4), kind=kOutput, calls=%fused_computation.8 | convolution fusion | flops 2217000960 | bytes 9994240 | tf_op jit(solution)/shard_map/dot_general | solution.py:114
  242.2 3.6 %reshape.156 = bf16[32,12,2048]{2,1,0:T(8,128)(2,1)} reshape(bf16[384,2048]{1,0:T(8,128)(2,1)} %fusion.6) | data formatting | bytes 3145728 | tf_op jit(solution)/shard_map/reshape | solution.py:115
  245.8 6.9 %all-to-all-start.2 = ((bf16[32,12,2048]{2,1,0:T(8,128)(2,1)}), bf16[32,12,2048]{2,1,0:T(8,128)(2,1)}, u32[]{:S(2)}, u32[]{:S(2)}) async-start(bf16[32,12,2048]{2,1,0:T(8,128)(2,1)} %reshape.156), calls=%async_computation.2 | async-start | bytes 4194304 | tf_op jit(solution)/shard_map/all_to_all | solution.py:116
  252.8 0.1 convert_element_type.87
  252.9 0.1 reshape.161
  253.1 1.2 fusion.55
  254.4 0.1 copy.47
  254.5 49.1 %all-to-all-done.2 = bf16[32,12,2048]{2,1,0:T(8,128)(2,1)} async-done(((bf16[32,12,2048]{2,1,0:T(8,128)(2,1)}), bf16[32,12,2048]{2,1,0:T(8,128)(2,1)}, u32[]{:S(2)}, u32[]{:S(2)}) %all-to-all-start.2) | async-done | bytes 1572896 | tf_op jit(solution)/shard_map/all_to_all | solution.py:116
  303.5 3.6 %reshape.157 = bf16[384,2048]{1,0:T(8,128)(2,1)} reshape(bf16[32,12,2048]{2,1,0:T(8,128)(2,1)} %all-to-all-done.2) | data formatting | bytes 3145728 | tf_op jit(solution)/shard_map/reshape | solution.py:117
  307.1 6.7 %gather_fusion = bf16[384,2048]{1,0:T(8,128)(2,1)} fusion(bf16[384,2048]{1,0:T(8,128)(2,1)} %reshape.157, s32[1024]{0:T(1024)S(1)} %pad_clamp_fusion), kind=kCustom, calls=%fused_computation | custom fusion | bytes 3147264 | tf_op jit(solution)/shard_map/gather | solution.py:117
  313.8 3.9 %reshape.168 = f32[64,6,2048]{2,1,0:T(8,128)} reshape(bf16[384,2048]{1,0:T(8,128)(2,1)} %gather_fusion) | data formatting | bytes 4718592 | tf_op jit(solution)/shard_map/convert_element_type | solution.py:118
  317.7 3.7 %multiply_reduce_fusion = f32[64,2048]{1,0:T(8,128)S(1)} fusion(f32[64,6,2048]{2,1,0:T(8,128)} %reshape.168, f32[64,6]{1,0:T(8,128)S(1)} %copy.47), kind=kLoop, calls=%fused_computation.1 | loop fusion | flops 1441792 | bytes 3671552 | tf_op jit(solution)/shard_map/reduce_sum | solution.py:118
  321.5 0.8 fusion.27
  (18 shorter events, 0.2 us)
Async XLA Ops:
  7.2 228.3 %copy-start = (bf16[1,704,2048]{2,1,0:T(8,128)(2,1)S(1)}, bf16[1,704,2048]{2,1,0:T(8,128)(2,1)}, u32[]{:S(2)}) copy-start(bf16[1,704,2048]{2,1,0:T(8,128)(2,1)} %param.29) | copy-start | bytes 8650756
  7.2 24.8 %copy-start.4 = (s32[1,64,6]{1,0,2:T(1,128)S(1)}, s32[1,64,6]{1,0,2:T(1,128)}, u32[]{:S(2)}) copy-start(s32[1,64,6]{1,0,2:T(1,128)} %param.26) | copy-start | bytes 4612
  7.2 28.0 %copy-start.1 = (bf16[1,64,8,512]{3,2,1,0:T(8,128)(2,1)S(1)}, bf16[1,64,8,512]{3,2,1,0:T(8,128)(2,1)}, u32[]{:S(2)}) copy-start(bf16[1,64,8,512]{3,2,1,0:T(8,128)(2,1)} %param.16) | copy-start | bytes 1572868
  7.2 150.4 %all-gather.2.cloned.1.call-start = ((), (), s32[]{:S(2)}) async-start(), calls=%async_computation.3 | async-start | bytes 4325376 | tf_op jit(solution)/shard_map/all_gather | solution.py:80
  8.8 27.6 %copy-start.3 = (bf16[1,64,64]{2,1,0:T(8,128)(2,1)S(1)}, bf16[1,64,64]{2,1,0:T(8,128)(2,1)}, u32[]{:S(2)}) copy-start(bf16[1,64,64]{2,1,0:T(8,128)(2,1)} %param.21) | copy-start | bytes 24580
  10.0 69.4 %all-to-all-start = ((bf16[32,16,8,128]{3,1,2,0:T(8,128)(2,1)}), bf16[32,16,8,128]{3,1,2,0:T(8,128)(2,1)}, u32[]{:S(2)}, u32[]{:S(2)}) async-start(bf16[32,16,8,128]{3,1,2,0:T(8,128)(2,1)} %broadcast_in_dim.15), calls=%async_computation | async-start | bytes 2097152 | tf_op jit(solution)/shard_map/all_to_all | solution.py:18
  81.9 78.9 %copy-start.2 = (f32[2048]{0:T(1024)S(1)}, f32[2048]{0:T(1024)}, u32[]{:S(2)}) copy-start(f32[2048]{0:T(1024)} %param.24) | copy-start | bytes 24580
  245.8 7.1 %copy-start.5 = (s32[1,64,6]{1,0,2:T(1,128)S(1)}, s32[1,64,6]{1,0,2:T(1,128)}, u32[]{:S(2)}) copy-start(s32[1,64,6]{1,0,2:T(1,128)} %param.26) | copy-start | bytes 4612
  245.8 57.7 %all-to-all-start.2 = ((bf16[32,12,2048]{2,1,0:T(8,128)(2,1)}), bf16[32,12,2048]{2,1,0:T(8,128)(2,1)}, u32[]{:S(2)}, u32[]{:S(2)}) async-start(bf16[32,12,2048]{2,1,0:T(8,128)(2,1)} %reshape.156), calls=%async_computation.2 | async-start | bytes 4194304 | tf_op jit(solution)/shard_map/all_to_all | solution.py:116
Sparse Core Ops, SparseCore 0:
  12.3 145.1 all-gather.1
where the time goes:
time: 331 us; the launch traced here: 329 us
  waiting for transfers between devices  166 us (50%)
  blocking collectives  60.7 us (18%)
  local copies, waits for them, and re-layouts  30.2 us (9%)
  starting transfers between devices  28.9 us (9%)
  matrix products  22.4 us (7%)
  between operations  14.2 us (4%)
  other arithmetic  6.66 us (2%)
    all_gather x1, waiting for transfers between devices, per_device(): lax.all_gather(w_out, 'fsdp', axis=0, tiled=True)  75.7 us
    all_to_all x1, blocking collectives, per_device(): lax.all_to_all(buffers, 'ep', split_axis=0, concat_axis=0, tiled=True)  60.7 us
    all_to_all x1, waiting for transfers between devices, per_device(): lax.all_to_all(result, 'ep', split_axis=0, concat_axis=0, tiled=True)  49.1 us
    all_to_all x1, waiting for transfers between devices, from_everyone(): return lax.all_to_all(copies, axis, split_axis=0, concat_axis=0, tiled=True)  40.6 us
    all_to_all x1, starting transfers between devices, from_everyone(): return lax.all_to_all(copies, axis, split_axis=0, concat_axis=0, tiled=True)  21.9 us
    all_to_all x1, starting transfers between devices, per_device(): lax.all_to_all(result, 'ep', split_axis=0, concat_axis=0, tiled=True)  6.93 us
    dot_general x1, matrix products, per_device(): jnp.dot(activated, w_down[0], preferred_element_type=jnp.float32)  6.77 us
    gather x1, local copies, waits for them, and re-layouts, per_device(): returned_rows = returned.reshape(expert_count * capacity, -1)[target]  6.67 us
  transfers between devices with their start and end apart: 3, of which 3 were waited for; matrix products, arithmetic and copies ran while one was open for 4% of the time, Pallas kernels for 0%

commit v1 on v0

v1 whole, which is shorter than its diff:
```python
import jax
import jax.numpy as jnp
from jax import lax
from jax.experimental import pallas as pl
from jax.experimental.pallas import tpu as pltpu
from jax.sharding import PartitionSpec as P

softmax_scale = 0.07216878364870323
epsilon = 1e-06
MESH = pl.DeviceIdType.MESH
F32 = jnp.float32
BF = jnp.bfloat16
C = 4
W = 512
CAP = 12
RY = 8


def iota(shape, dim):
    return lax.broadcasted_iota(jnp.int32, shape, dim)


def dot(a, b):
    return jnp.dot(a, b, preferred_element_type=F32)


def dot_t(a, b):
    return lax.dot_general(a, b, (((1,), (1,)), ((), ())), preferred_element_type=F32)


def kernel(
    x_ref, q_ref, qr_ref, cl_ref, cr_ref, nl_ref, nr_ref, wuv_ref, wout_ref, gain_ref, router_ref,
    ids_ref, wg_hbm, wu_hbm, wd_hbm,
    att_ref, out_ref,
    G, wg, wu, wd, KL, KR, MX, HF, HB, NB, MB, WT, SEL, SX, XB, AG, AU, ACT, OB, RB, PS, SB, YB,
    wsem, gz, gx2, gx, gy, gc, ay, am, zf, zb, rs,
):
    f = lax.axis_index("fsdp")
    ep = lax.axis_index("ep")
    x, zh, c = f // 8, (f // 2) % 4, f % 2
    y, zl = ep // 4, ep % 4
    z = zh * 4 + zl

    def dev(dx=0, dy=0, dz=0, dc=0):
        nx, ny, nz, nc = (x + dx + 4) % 4, (y + dy + RY) % RY, (z + dz + 16) % 16, (c + dc) % 2
        return (nx * 8 + (nz // 4) * 2 + nc, ny * 4 + nz % 4)

    sent = []

    def copy(src, dst, sems, idx, to):
        return pltpu.make_async_remote_copy(
            src_ref=src, dst_ref=dst, send_sem=sems.at[(0, *idx)], recv_sem=sems.at[(1, *idx)],
            device_id=to, device_id_type=MESH,
        )

    def send(src, dst, sems, idx, to):
        cp = copy(src, dst, sems, idx, to)
        cp.start()
        sent.append(cp)

    def recv(dst, sems, idx):
        copy(dst, dst, sems, idx, dev(dy=1)).wait_recv()

    two = 2 - 4 * c
    partners = [
        dev(dy=1), dev(dy=-1), dev(dz=1), dev(dz=-1), dev(dz=2), dev(dz=-2), dev(dc=1),
        dev(dx=1), dev(dx=-1), dev(dx=2), dev(dz=4), dev(dz=-4), dev(dz=8),
    ]
    barrier = pltpu.get_barrier_semaphore()
    for to in partners:
        pl.semaphore_signal(barrier, inc=1, device_id=to, device_id_type=MESH)
    loads = [
        pltpu.make_async_copy(wg_hbm, wg, wsem.at[0]),
        pltpu.make_async_copy(wu_hbm, wu, wsem.at[1]),
        pltpu.make_async_copy(wd_hbm, wd, wsem.at[2]),
    ]
    for ld in loads:
        ld.start()
    mine = x * 4 + zh
    G[y, mine, c, 0:16] = wuv_ref[:, pl.ds(pl.multiple_of(y * 128, 128), 128)]
    G[y, mine, c, 16:48] = wout_ref[:, pl.ds(pl.multiple_of(y * 128, 128), 128)]
    G[y, mine, c, 48:80] = wout_ref[:, pl.ds(pl.multiple_of(1024 + y * 128, 128), 128)]
    pl.semaphore_wait(barrier, len(partners))

    own = G.at[y, mine, c]
    for d in range(1, 4):
        send(own, own, gz, (d - 1,), dev(dz=4 * d))

    KL[0:64] = cl_ref[...]
    KL[64:128] = nl_ref[...]
    KR[0:64] = cr_ref[...]
    KR[64:128] = nr_ref[...]
    scores = (dot_t(q_ref[...], KL[...]) + dot_t(qr_ref[...], KR[...])) * softmax_scale
    visible = iota((512, 128), 1) <= (iota((512, 128), 0) >> 3) + 64
    top = jnp.max(jnp.where(visible, scores, -jnp.inf), axis=1, keepdims=True)
    expo = jnp.where(visible, jnp.exp(scores - top), 0.0)
    probs = (expo / jnp.sum(expo, axis=1, keepdims=True)).astype(BF)
    r, cc = iota((512, 512), 0), iota((512, 512), 1)
    perm = jnp.where(cc == ((r & 63) << 3) + (r >> 6), 1.0, 0.0).astype(BF)
    probs = dot(perm, probs).astype(BF)
    MX[...] = dot(probs, KL[...]).astype(BF)

    x2 = (x + 2) % 4

    def unit(j, xx, cx):
        return G.at[j, pl.ds(4 * xx, 4), cx]

    def to_core(j, xx, s, slot):
        u = unit(j, xx, c)
        send(u, u, gc, (s, slot), dev(dc=1))

    def to_x(j, s):
        u = unit(j, x, c)
        send(u, u, gx, (0, s), dev(dx=1))
        send(u, u, gx, (1, s), dev(dx=-1))

    def ring(j, xx, kind, way, s):
        u = unit(j, xx, c)
        send(u, u, gy, (kind, way, s), dev(dy=1 if way == 0 else -1))

    def piece(way, s):
        return (y - s + RY) % RY if way == 0 else (y + s) % RY

    def number(way, s):
        return 0 if s == 0 else (s if way == 0 else 4 + s)

    steps = [[4, 3], [3, 4]]
    for d in range(1, 4):
        recv(own, gz, (d - 1,))
    u0 = unit(y, x, c)
    send(u0, u0, gx2, (0,), dev(dx=2))
    for way in range(2):
        ring(y, x, 0, way, 0)
    to_x(y, 0)
    to_core(y, x, 0, 0)
    recv(unit(y, x2, c), gx2, (0,))
    for way in range(2):
        ring(y, x2, 1, way, 0)
    to_core(y, x2, 0, 1)

    def took_x(j, s):
        for i, xx in ((0, (x + 3) % 4), (1, (x + 1) % 4)):
            recv(unit(j, xx, c), gx, (i, s))
            to_core(j, xx, s, 2 + i)

    def slot_of(way, s, kind):
        return s if way == 0 else RY - s

    for s in range(1, 5):
        for kind in range(2):
            xx = x if kind == 0 else x2
            for way in range(2):
                if s > steps[kind][way]:
                    continue
                j = piece(way, s)
                recv(unit(j, xx, c), gy, (kind, way, s - 1))
                if s < steps[kind][way]:
                    ring(j, xx, kind, way, s)
                n = slot_of(way, s, kind)
                if kind == 0:
                    to_x(j, n)
                to_core(j, xx, n, kind)
        if s == 1:
            took_x(y, 0)
        else:
            for way in range(2):
                took_x(piece(way, s - 1), slot_of(way, s - 1, 0))
    took_x(piece(0, 4), 4)
    o = 1 - c
    for n in range(RY):
        j = (y - n + RY) % RY
        for slot, xx in ((0, x), (1, x2), (2, (x + 3) % 4), (3, (x + 1) % 4)):
            recv(unit(j, xx, o), gc, (n, slot))

    for h in range(8):
        w = G[h, :, :, 0:16].reshape(512, 128)
        HF[:, 128 * h : 128 * (h + 1)] = dot(MX[64 * h : 64 * (h + 1)], w).astype(BF)
    heads = HF[...]
    square = jnp.zeros((64, 1), F32)
    for half in range(2):
        for j in range(8):
            w = G[j, :, :, 16 + 32 * half : 48 + 32 * half].reshape(1024, 128)
            cols = slice(1024 * half + 128 * j, 1024 * half + 128 * (j + 1))
            hid = x_ref[:, cols].astype(F32) + dot(heads, w)
            HB[:, cols] = hid
            att_ref[:, cols] = hid.astype(BF)
            square = square + jnp.sum(hid * hid, axis=1, keepdims=True)
    inv = lax.rsqrt(square * (1.0 / 2048) + epsilon)
    for k in range(C):
        cols = slice(W * k, W * (k + 1))
        NB[k, y] = (HB[:, cols] * inv * gain_ref[:, cols]).astype(BF)

    far = [[4, 3], [3, 4], [4, 3], [3, 4]]

    def tok(k, way, s):
        b = NB.at[k, piece(way, s)]
        send(b, b, ay, (k, way, s), dev(dy=1 if way == 0 else -1))

    def met(way, s):
        b = MB.at[piece(way, s)]
        send(b, b, am, (way, s), dev(dy=1 if way == 0 else -1))

    for way in range(2):
        tok(0, way, 0)
    logits = jnp.zeros((64, 32), F32)
    for k in range(C):
        logits = logits + dot(NB[k, y], router_ref[W * k : W * (k + 1)])
    e32 = iota((64, 32), 1)
    choose = jnp.zeros((64, 32), F32)
    for k in range(6):
        choose = choose + jnp.where(ids_ref[:, k : k + 1] == e32, 1.0, 0.0)
    chosen = choose > 0.5
    ltop = jnp.max(jnp.where(chosen, logits, -jnp.inf), axis=1, keepdims=True)
    gexp = jnp.where(chosen, jnp.exp(logits - ltop), 0.0)
    gate = gexp / jnp.sum(gexp, axis=1, keepdims=True)
    lower = jnp.where(iota((64, 64), 1) < iota((64, 64), 0), 1.0, 0.0).astype(BF)
    rank = dot(lower, choose.astype(BF))
    rank = jnp.where(chosen, rank, -1.0)
    e0 = jnp.where(iota((32, 128), 0) == iota((32, 128), 1), 1.0, 0.0).astype(BF)
    e1 = jnp.where(iota((32, 128), 0) + 32 == iota((32, 128), 1), 1.0, 0.0).astype(BF)
    MB[y] = (dot(rank.astype(BF), e0) + dot(gate.astype(BF), e1)).astype(BF)
    for way in range(2):
        met(way, 0)

    offs = [0, 1, -1, two]

    def plan():
        lane = iota((64, 128), 1)
        for i in range(4):
            e = 4 * y + (zl + offs[i] + 4) % 4
            for j in range(RY):
                m = MB[j].astype(F32)
                a = jnp.sum(jnp.where(lane == e, m, 0.0), axis=1, keepdims=True)
                g = jnp.sum(jnp.where(lane == e + 32, m, 0.0), axis=1, keepdims=True)
                hit = (a > -0.5) & (lane.astype(F32) == a + float(CAP * j))
                HOT = jnp.where(hit, 1.0, 0.0)
                WT[i, 64 * j : 64 * (j + 1)] = jnp.where(hit, g, 0.0).astype(BF)
                PS[0, j, :, 128 * i : 128 * (i + 1)] = HOT
        for i in range(4):
            hot = PS[0, :, :, 128 * i : 128 * (i + 1)].reshape(512, 128)
            SEL[i] = hot.T.astype(BF)

    def select(k):
        rows = NB[k].reshape(512, W)
        for i in (1, 2, 3, 0):
            picked = dot(SEL[i, 0:96], rows).astype(BF)
            if i == 0:
                XB[k, 0] = picked
            else:
                SX[k, i - 1] = picked
                send(SX.at[k, i - 1], XB.at[k, i], zf, (k, i - 1), dev(dz=offs[i]))

    def expert(k):
        for i in range(1, 4):
            recv(XB.at[k, i], zf, (k, i - 1))
        if k == 0:
            loads[0].wait()
            loads[1].wait()
        rows = XB[k].reshape(384, W)
        g = dot(rows, wg[W * k : W * (k + 1)])
        u = dot(rows, wu[W * k : W * (k + 1)])
        if k == 0:
            AG[...] = g
            AU[...] = u
        elif k < C - 1:
            AG[...] += g
            AU[...] += u
        else:
            g = AG[...] + g
            u = AU[...] + u
            ACT[...] = (g / (1.0 + jnp.exp(-g)) * u).astype(BF)

    for t in range(C + 5):
        for k in range(C):
            s = t - k
            for way in range(2):
                dist = far[k][way]
                if 1 <= s <= dist:
                    recv(NB.at[k, piece(way, s)], ay, (k, way, s - 1))
                if 0 <= s < dist and (k, s) != (0, 0):
                    tok(k, way, s)
            if k == 0:
                for way in range(2):
                    dist = far[0][way]
                    if 1 <= s <= dist:
                        recv(MB.at[piece(way, s)], am, (way, s - 1))
                    if 1 <= s < dist:
                        met(way, s)
        if t == 4:
            plan()
        if 0 <= t - 4 < C:
            select(t - 4)
        if 0 <= t - 5 < C:
            expert(t - 5)

    loads[2].wait()
    for k in range(C):
        OB[k] = dot(ACT[...], wd[:, W * k : W * (k + 1)]).astype(BF).reshape(4, 96, W)
        for i in range(1, 4):
            send(OB.at[k, i], RB.at[k, i], zb, (k, i - 1), dev(dz=-offs[i]))

    def own_sum(k):
        for i in range(1, 4):
            recv(RB.at[k, i], zb, (k, i - 1))
        total = dot(WT[0, :, 0:96], OB[k, 0])
        for i in range(1, 4):
            total = total + dot(WT[i, :, 0:96], RB[k, i])
        PS[k] = total.reshape(RY, 64, W)

    def take(k, way, s):
        b = YB.at[k, way, s - 1]
        recv(b, rs, (k, way, s - 1))
        return b[...].astype(F32)

    def final(k):
        cols = slice(W * k, W * (k + 1))
        total = HB[:, cols] + PS[k, y]
        for way in range(2):
            total = total + take(k, way, far[k][way])
        out_ref[:, cols] = total.astype(BF)

    for t in range(C + 5):
        if t < C:
            own_sum(t)
        for k in range(C):
            s = t - k
            for way in range(2):
                dist = far[k][way]
                if 0 <= s < dist:
                    dest = (y + dist - s) % RY if way == 0 else (y - dist + s + RY) % RY
                    val = PS[k, dest]
                    if s > 0:
                        val = val + take(k, way, s)
                    SB[k, way, s] = val.astype(BF)
                    send(
                        SB.at[k, way, s], YB.at[k, way, s], rs, (k, way, s),
                        dev(dy=1 if way == 0 else -1),
                    )
            if s == 4:
                final(k)
    for cp in sent:
        cp.wait_send()


def per_device(
    x_resid, q_latent, q_rope, cache_latent, cache_rope, new_latent, new_rope, w_uv, w_out,
    norm_gain, router, expert_ids, w_gate, w_up, w_down,
):
    vmem = pl.BlockSpec(memory_space=pltpu.VMEM)
    anyspace = pl.BlockSpec(memory_space=pl.ANY)
    dma = pltpu.SemaphoreType.DMA
    att, out = pl.pallas_call(
        kernel,
        out_shape=(jax.ShapeDtypeStruct((64, 2048), BF), jax.ShapeDtypeStruct((64, 2048), BF)),
        in_specs=[vmem] * 12 + [anyspace] * 3,
        out_specs=(vmem, vmem),
        scratch_shapes=[
            pltpu.VMEM((8, 16, 2, 80, 128), BF),
            pltpu.VMEM((2048, 704), BF),
            pltpu.VMEM((2048, 704), BF),
            pltpu.VMEM((704, 2048), BF),
            pltpu.VMEM((128, 512), BF),
            pltpu.VMEM((128, 64), BF),
            pltpu.VMEM((512, 512), BF),
            pltpu.VMEM((64, 1024), BF),
            pltpu.VMEM((64, 2048), F32),
            pltpu.VMEM((C, RY, 64, W), BF),
            pltpu.VMEM((RY, 64, 128), BF),
            pltpu.VMEM((4, 512, 128), BF),
            pltpu.VMEM((4, 128, 512), BF),
            pltpu.VMEM((C, 3, 96, W), BF),
            pltpu.VMEM((C, 4, 96, W), BF),
            pltpu.VMEM((384, 704), F32),
            pltpu.VMEM((384, 704), F32),
            pltpu.VMEM((384, 704), BF),
            pltpu.VMEM((C, 4, 96, W), BF),
            pltpu.VMEM((C, 4, 96, W), BF),
            pltpu.VMEM((C, RY, 64, W), F32),
            pltpu.VMEM((C, 2, 4, 64, W), BF),
            pltpu.VMEM((C, 2, 4, 64, W), BF),
            dma((3,)),
            dma((2, 3)),
            dma((2, 1)),
            dma((2, 2, RY)),
            dma((2, 2, 2, 4)),
            dma((2, RY, 4)),
            dma((2, C, 2, 4)),
            dma((2, 2, 4)),
            dma((2, C, 3)),
            dma((2, C, 3)),
            dma((2, C, 2, 4)),
        ],
        compiler_params=pltpu.CompilerParams(
            collective_id=0, has_side_effects=True, vmem_limit_bytes=56 << 20
        ),
    )(
        x_resid[0],
        q_latent.reshape(512, 512),
        q_rope.reshape(512, 64),
        cache_latent[0],
        cache_rope[0],
        new_latent[0],
        new_rope[0],
        w_uv.reshape(16, 1024),
        w_out,
        norm_gain.reshape(1, 2048),
        router,
        expert_ids[0],
        w_gate[0],
        w_up[0],
        w_down[0],
    )
    return att[None], out[None]


def solution(mesh):
    seq = P(("fsdp", "ep"), None, None)
    placed = (
        seq,
        P(("fsdp", "ep"), None, None, None),
        P(("fsdp", "ep"), None, None, None),
        seq,
        seq,
        seq,
        seq,
        P("fsdp", None, None),
        P("fsdp", None),
        P(),
        P(),
        seq,
        P("ep", None, None),
        P("ep", None, None),
        P("ep", None, None),
    )
    return jax.shard_map(
        per_device, mesh=mesh, in_specs=placed, out_specs=(seq, seq), check_vma=False
    )
```

time: 331 us -> 160 us (0.48)
  waiting for transfers between devices: 166 us -> 0 us
  Pallas kernels: 0 us -> 143 us
  blocking collectives: 60.7 us -> 0 us
  starting transfers between devices: 28.9 us -> 0 us
  matrix products: 22.4 us -> 0 us
  local copies, waits for them, and re-layouts: 30.2 us -> 15.6 us
  between operations: 14.2 us -> 0.64 us
  other arithmetic: 6.66 us -> 0 us
    pallas_call x0 -> x1, Pallas kernels: none -> 143 us  [per_device(): pl.pallas_call(kernel, out_shape=(jax.ShapeDtypeStruct((64, 2048), BF), j...]
    all_to_all x2 -> x0, waiting for transfers between devices: 89.7 us -> none  [the longest x1 49.1 us: per_device(): lax.all_to_all(result, 'ep', split_axis=0, concat_axis=0, tiled=True)]
    all_gather x1 -> x0, waiting for transfers between devices: 75.7 us -> none  [per_device(): lax.all_gather(w_out, 'fsdp', axis=0, tiled=True)]
    all_to_all x1 -> x0, blocking collectives: 60.7 us -> none  [per_device(): lax.all_to_all(buffers, 'ep', split_axis=0, concat_axis=0, tiled=True)]
    all_to_all x2 -> x0, starting transfers between devices: 28.8 us -> none  [the longest x1 21.9 us: from_everyone(): return lax.all_to_all(copies, axis, split_axis=0, concat_axis=0, tiled=True)]
    dot_general x9 -> x0, matrix products: 22.4 us -> none  [the longest x1 6.77 us: per_device(): jnp.dot(activated, w_down[0], preferred_element_type=jnp.float32)]
    unnamed x14 -> x9, local copies, waits for them, and re-layouts: 0.96 us -> 15.6 us
    reshape x4 -> x0, local copies, waits for them, and re-layouts: 14.4 us -> none  [the longest x1 3.64 us: per_device(): buffer_rows = received.reshape(source_count * slot_count, width)]
  transfers between devices with their start and end apart: 3 -> 0, of which waited for: 3 -> 0; matrix products, arithmetic and copies ran while one was open for 4% -> 0% of each run, Pallas kernels for 0% -> 0%
where the time goes in v1:
time: 160 us; the launch traced here: 159 us
  Pallas kernels  143 us (89%)
  local copies, waits for them, and re-layouts  15.6 us (10%)
    pallas_call x1, Pallas kernels, per_device(): pl.pallas_call(kernel, out_shape=(jax.ShapeDtypeStruct((64, 2048), BF), j...  143 us
    unnamed x9, local copies, waits for them, and re-layouts  15.6 us

profile of v1, /device:TPU:6, one launch (start us, length us, event | category | flops | bytes accessed | tf_op | source)
XLA Modules:
  0.0 159.2 jit_solution(5504143891234637493)
XLA Ops:
  0.6 1.4 copy.23
  2.0 1.4 copy.17
  3.4 1.9 %copy.20.router_ref = bf16[2048,32]{1,0:T(8,128)(2,1)} copy(bf16[2048,32]{0,1:T(8,128)(2,1)} %param.25) | data formatting | bytes 262144 | tf_op args[10]
  5.3 0.0 copy-start
  5.3 4.7 %copy.18 = bf16[1,2048,704]{2,1,0:T(8,128)(2,1)} copy(bf16[1,2048,704]{1,2,0:T(8,128)(2,1)} %param.27) | data formatting | bytes 5767168 | tf_op args[12]
  10.0 0.0 copy-done
  10.1 2.8 %copy.19 = bf16[1,2048,704]{2,1,0:T(8,128)(2,1)} copy(bf16[1,2048,704]{1,2,0:T(8,128)(2,1)S(1)} %copy-done) | data formatting | bytes 5767168 | tf_op args[13]
  12.9 143.0 %shard_map.158 = (bf16[64,2048]{1,0:T(8,128)(2,1)}, bf16[64,2048]{1,0:T(8,128)(2,1)}) custom-call(bf16[64,2048]{1,0:T(8,128)(2,1)} %bitcast.22, bf16[512,512]{1,0:T(8,128)(2,1)} %bitcast.21, bf16[512,64]{1,0:T(8,128)(2,1)} %bitcast.25, bf16[64,512]{1,0:T(8,128)(2,1)} %bitcast.28, bf16[64,64]{1,0:T(8,128)(2,1)} %bitcast.31, bf16[64,512]{1,0:T(8,128)(2,1)} %bitcast.29, ...), custom_call_target="tpu_custom_call" | custom-call | tf_op jit(solution)/shard_map/pallas_call | solution.py:352
  155.8 1.7 %copy.26 = bf16[1,64,2048]{2,1,0:T(8,128)(2,1)} copy(bf16[1,64,2048]{2,1,0:T(8,128)(2,1)} %bitcast.24) | data formatting | bytes 524288
  157.5 1.7 %copy.27 = bf16[1,64,2048]{2,1,0:T(8,128)(2,1)} copy(bf16[1,64,2048]{2,1,0:T(8,128)(2,1)} %bitcast.23) | data formatting | bytes 524288
Async XLA Ops:
  5.3 4.7 %copy-start = (bf16[1,2048,704]{1,2,0:T(8,128)(2,1)S(1)}, bf16[1,2048,704]{1,2,0:T(8,128)(2,1)}, u32[]{:S(2)}) copy-start(bf16[1,2048,704]{1,2,0:T(8,128)(2,1)} %param.28) | copy-start | bytes 8650756

commit v2 on v1

v2 whole, which is shorter than its diff:
```python
import jax
import jax.numpy as jnp
from jax import lax
from jax.experimental import pallas as pl
from jax.experimental.pallas import tpu as pltpu
from jax.sharding import PartitionSpec as P

softmax_scale = 0.07216878364870323
epsilon = 1e-06
MESH = pl.DeviceIdType.MESH
F32 = jnp.float32
BF = jnp.bfloat16
C = 4
W = 512
PAD = 16
RY = 8


def iota(shape, dim):
    return lax.broadcasted_iota(jnp.int32, shape, dim)


def dot(a, b):
    return jnp.dot(a, b, preferred_element_type=F32)


def dot_t(a, b):
    return lax.dot_general(a, b, (((1,), (1,)), ((), ())), preferred_element_type=F32)


def kernel(
    x_ref, q_ref, qr_ref, cl_ref, cr_ref, nl_ref, nr_ref, wuv_ref, wout_ref, gain_ref, router_ref,
    ids_ref, wg_hbm, wu_hbm, wd_hbm,
    att_ref, out_ref,
    G, wg, wu, wd, KL, KR, PR, MX, HF, HB, NB, MB, WT, X3, SX, XB, OB, RB, PS, SB, YB,
    wsem, gz, gx2, gx, gy, gc, ay, am, zf, zb, rs,
):
    f = lax.axis_index("fsdp")
    ep = lax.axis_index("ep")
    x, zh, c = f // 8, (f // 2) % 4, f % 2
    y, zl = ep // 4, ep % 4
    z = zh * 4 + zl

    def dev(dx=0, dy=0, dz=0, dc=0):
        nx, ny, nz, nc = (x + dx + 4) % 4, (y + dy + RY) % RY, (z + dz + 16) % 16, (c + dc) % 2
        return (nx * 8 + (nz // 4) * 2 + nc, ny * 4 + nz % 4)

    sent = []

    def copy(src, dst, sems, idx, to):
        return pltpu.make_async_remote_copy(
            src_ref=src, dst_ref=dst, send_sem=sems.at[(0, *idx)], recv_sem=sems.at[(1, *idx)],
            device_id=to, device_id_type=MESH,
        )

    def send(src, dst, sems, idx, to):
        cp = copy(src, dst, sems, idx, to)
        cp.start()
        sent.append(cp)

    def recv(dst, sems, idx):
        copy(dst, dst, sems, idx, dev(dy=1)).wait_recv()

    two = 2 - 4 * c
    partners = [
        dev(dy=1), dev(dy=-1), dev(dz=1), dev(dz=-1), dev(dz=2), dev(dz=-2), dev(dc=1),
        dev(dx=1), dev(dx=-1), dev(dx=2), dev(dz=4), dev(dz=-4), dev(dz=8),
    ]
    barrier = pltpu.get_barrier_semaphore()
    for to in partners:
        pl.semaphore_signal(barrier, inc=1, device_id=to, device_id_type=MESH)
    loads = [
        pltpu.make_async_copy(wg_hbm, wg, wsem.at[0]),
        pltpu.make_async_copy(wu_hbm, wu, wsem.at[1]),
        pltpu.make_async_copy(wd_hbm, wd, wsem.at[2]),
    ]
    for ld in loads:
        ld.start()
    mine = x * 4 + zh
    wuv = jnp.where(iota((16, 8, 128), 1) == y, wuv_ref[...].astype(F32), 0.0)
    G[y, mine, c, 0:16] = jnp.sum(wuv, axis=1).astype(BF)
    G[y, mine, c, 16:48] = wout_ref[:, pl.ds(pl.multiple_of(y * 128, 128), 128)]
    G[y, mine, c, 48:80] = wout_ref[:, pl.ds(pl.multiple_of(1024 + y * 128, 128), 128)]
    pl.semaphore_wait(barrier, len(partners))

    own = G.at[y, mine, c]
    for d in range(1, 4):
        send(own, own, gz, (d - 1,), dev(dz=4 * d))

    def attend(n):
        if n == 0:
            KL[0:64] = cl_ref[...]
            KL[64:128] = nl_ref[...]
            KR[0:64] = cr_ref[...]
            KR[64:128] = nr_ref[...]
        rows = slice(128 * n, 128 * (n + 1))
        scores = (dot_t(q_ref[rows], KL[...]) + dot_t(qr_ref[rows], KR[...])) * softmax_scale
        visible = iota((128, 128), 1) <= ((iota((128, 128), 0) + 128 * n) >> 3) + 64
        top = jnp.max(jnp.where(visible, scores, -jnp.inf), axis=1, keepdims=True)
        expo = jnp.where(visible, jnp.exp(scores - top), 0.0)
        PR[rows] = (expo / jnp.sum(expo, axis=1, keepdims=True)).astype(BF)

    def mix(n):
        r, cc = iota((128, 512), 0) + 128 * n, iota((128, 512), 1)
        perm = jnp.where(cc == ((r & 63) << 3) + (r >> 6), 1.0, 0.0).astype(BF)
        part = dot(perm, PR[...]).astype(BF)
        MX[128 * n : 128 * (n + 1)] = dot(part, KL[...]).astype(BF)

    for n in range(2):
        attend(n)

    x2 = (x + 2) % 4

    def unit(j, xx, cx):
        return G.at[j, pl.ds(4 * xx, 4), cx]

    def to_core(j, xx, s, slot):
        u = unit(j, xx, c)
        send(u, u, gc, (s, slot), dev(dc=1))

    def to_x(j, s):
        u = unit(j, x, c)
        send(u, u, gx, (0, s), dev(dx=1))
        send(u, u, gx, (1, s), dev(dx=-1))

    def ring(j, xx, kind, way, s):
        u = unit(j, xx, c)
        send(u, u, gy, (kind, way, s), dev(dy=1 if way == 0 else -1))

    def piece(way, s):
        return (y - s + RY) % RY if way == 0 else (y + s) % RY

    def number(way, s):
        return 0 if s == 0 else (s if way == 0 else 4 + s)

    steps = [[4, 3], [3, 4]]
    for d in range(1, 4):
        recv(own, gz, (d - 1,))
    u0 = unit(y, x, c)
    send(u0, u0, gx2, (0,), dev(dx=2))
    for way in range(2):
        ring(y, x, 0, way, 0)
    for n in range(2, 4):
        attend(n)
    recv(unit(y, x2, c), gx2, (0,))
    for way in range(2):
        ring(y, x2, 1, way, 0)
    to_x(y, 0)
    to_core(y, x, 0, 0)
    to_core(y, x2, 0, 1)

    def took_x(j, s):
        for i, xx in ((0, (x + 3) % 4), (1, (x + 1) % 4)):
            recv(unit(j, xx, c), gx, (i, s))
            to_core(j, xx, s, 2 + i)

    def slot_of(way, s, kind):
        return s if way == 0 else RY - s

    for s in range(1, 5):
        for kind in range(2):
            xx = x if kind == 0 else x2
            for way in range(2):
                if s > steps[kind][way]:
                    continue
                j = piece(way, s)
                recv(unit(j, xx, c), gy, (kind, way, s - 1))
                if s < steps[kind][way]:
                    ring(j, xx, kind, way, s)
                n = slot_of(way, s, kind)
                if kind == 0:
                    to_x(j, n)
                to_core(j, xx, n, kind)
        mix(s - 1)
        if s == 1:
            took_x(y, 0)
        else:
            for way in range(2):
                took_x(piece(way, s - 1), slot_of(way, s - 1, 0))
    took_x(piece(0, 4), 4)
    o = 1 - c
    for n in range(RY):
        j = (y - n + RY) % RY
        for slot, xx in ((0, x), (1, x2), (2, (x + 3) % 4), (3, (x + 1) % 4)):
            recv(unit(j, xx, o), gc, (n, slot))

    for h in range(8):
        w = G[h, :, :, 0:16].reshape(512, 128)
        HF[:, 128 * h : 128 * (h + 1)] = dot(MX[64 * h : 64 * (h + 1)], w).astype(BF)
    heads = HF[...]
    square = jnp.zeros((64, 1), F32)
    for half in range(2):
        for j in range(8):
            w = G[j, :, :, 16 + 32 * half : 48 + 32 * half].reshape(1024, 128)
            cols = slice(1024 * half + 128 * j, 1024 * half + 128 * (j + 1))
            hid = x_ref[:, cols].astype(F32) + dot(heads, w)
            HB[:, cols] = hid
            att_ref[:, cols] = hid.astype(BF)
            square = square + jnp.sum(hid * hid, axis=1, keepdims=True)
    inv = lax.rsqrt(square * (1.0 / 2048) + epsilon)
    for k in range(C):
        cols = slice(W * k, W * (k + 1))
        NB[y, k] = (HB[:, cols] * inv * gain_ref[:, cols]).astype(BF)

    far = [[4, 3], [3, 4], [4, 3], [3, 4]]

    def tok(k, way, s):
        b = NB.at[piece(way, s), k]
        send(b, b, ay, (k, way, s), dev(dy=1 if way == 0 else -1))

    def met(way, s):
        b = MB.at[piece(way, s)]
        send(b, b, am, (way, s), dev(dy=1 if way == 0 else -1))

    for k in range(C):
        for way in range(2):
            tok(k, way, 0)
    logits = jnp.zeros((64, 32), F32)
    for k in range(C):
        logits = logits + dot_t(NB[y, k], router_ref[:, W * k : W * (k + 1)])
    choose_t = jnp.zeros((32, 64), F32)
    for k in range(6):
        choose_t = choose_t + jnp.where(ids_ref[k] == iota((32, 64), 0), 1.0, 0.0)
    eye = jnp.where(iota((64, 64), 1) == iota((64, 64), 0), 1.0, 0.0).astype(BF)
    choose = dot_t(eye, choose_t.astype(BF))
    chosen = choose > 0.5
    ltop = jnp.max(jnp.where(chosen, logits, -jnp.inf), axis=1, keepdims=True)
    gexp = jnp.where(chosen, jnp.exp(logits - ltop), 0.0)
    gate = gexp / jnp.sum(gexp, axis=1, keepdims=True)
    lower = jnp.where(iota((64, 64), 1) < iota((64, 64), 0), 1.0, 0.0).astype(BF)
    rank = dot(lower, choose.astype(BF))
    rank = jnp.where(chosen, rank, -1.0)
    e0 = jnp.where(iota((32, 128), 0) == iota((32, 128), 1), 1.0, 0.0).astype(BF)
    e1 = jnp.where(iota((32, 128), 0) + 32 == iota((32, 128), 1), 1.0, 0.0).astype(BF)
    MB[y] = (dot(rank.astype(BF), e0) + dot(gate.astype(BF), e1)).astype(BF)
    for way in range(2):
        met(way, 0)

    offs = [0, 1, -1, two]
    order = [(0, 0), (0, 1), (1, 1), (0, 2), (1, 2), (0, 3), (1, 3), (0, 4)]

    def select(n):
        j = piece(*order[n])
        lane = iota((64, 128), 1)
        m = MB[j].astype(F32)
        hot = [jnp.zeros((64, 128), F32)] * 4
        weight = [jnp.zeros((64, 128), F32)] * 4
        for i in range(4):
            e = 4 * y + (zl + offs[i] + 4) % 4
            a = jnp.sum(jnp.where(lane == e, m, 0.0), axis=1, keepdims=True)
            g = jnp.sum(jnp.where(lane == e + 32, m, 0.0), axis=1, keepdims=True)
            for v in range(4):
                if v == 0:
                    hit = (a > -0.5) & (lane.astype(F32) == a + float(PAD * i))
                else:
                    d = a - float(4 * (v - 1))
                    hit = (d > -0.5) & (d < 3.5) & (lane.astype(F32) == d + float(PAD * i + 12))
                hot[v] = jnp.where(hit, 1.0, hot[v])
                weight[v] = jnp.where(hit, g, weight[v])
        sel = []
        for v in range(4):
            WT[n, v] = weight[v].astype(BF)
            sel.append(hot[v].T.astype(BF)[0:64])
        last = NB[j, 3]
        for k in range(3):
            cols = slice(W * k, W * (k + 1))
            picked = (dot(sel[0], NB[j, k]) + dot(sel[k + 1], last)).astype(BF)
            XB[n, 0, :, cols] = picked[0:PAD]
            for i in range(1, 4):
                SX[n, i - 1, :, cols] = picked[PAD * i : PAD * (i + 1)]
        for i in range(1, 4):
            send(SX.at[n, i - 1], XB.at[n, i], zf, (n, i - 1), dev(dz=offs[i]))

    def spread(q, back):
        r, cc = iota((64, 64), 1 if back else 0), iota((64, 64), 0 if back else 1)
        hit = ((r >> 4) == (cc >> 4)) & ((cc & 15) >= 12) & ((r & 15) == 4 * q + (cc & 15) - 12)
        return jnp.where(hit, 1.0, 0.0).astype(BF)

    def expert(lo, hi):
        for n in range(lo, hi):
            for i in range(1, 4):
                recv(XB.at[n, i], zf, (n, i - 1))
        if lo == 0:
            for ld in loads:
                ld.wait()
        count = (hi - lo) * 4 * PAD
        for n in range(lo, hi):
            tail = jnp.zeros((64, W), F32)
            for q in range(3):
                tail = tail + dot(spread(q, False), XB[n, :, :, W * q : W * (q + 1)].reshape(64, W))
            X3[n] = tail.astype(BF)
        rows = XB[lo:hi].reshape(count, 1536)
        tail = X3[lo:hi].reshape(count, W)
        g = dot_t(rows, wg[:, 0:1536]) + dot_t(tail, wg[:, 1536:2048])
        u = dot_t(rows, wu[:, 0:1536]) + dot_t(tail, wu[:, 1536:2048])
        act = (g / (1.0 + jnp.exp(-g)) * u).astype(BF)
        X3[lo:hi] = dot(act, wd[:, 1536:2048]).astype(BF).reshape(hi - lo, 64, W)
        front = (iota((64, W), 0) & 15) < 12
        for k in range(3):
            cols = slice(W * k, W * (k + 1))
            part = dot(act, wd[:, cols])
            for n in range(lo, hi):
                own_part = part[64 * (n - lo) : 64 * (n - lo + 1)]
                both = jnp.where(front, own_part, dot(spread(k, True), X3[n]))
                OB[n, :, :, cols] = both.astype(BF).reshape(4, PAD, W)
        for n in reversed(range(lo, hi)):
            for i in range(1, 4):
                send(OB.at[n, i], RB.at[n, i], zb, (n, i - 1), dev(dz=-offs[i]))

    def forward(s):
        for way in range(2):
            if s <= [4, 3][way]:
                recv(MB.at[piece(way, s)], am, (way, s - 1))
                if s < [4, 3][way]:
                    met(way, s)
        for k in range(C):
            for way in range(2):
                dist = far[k][way]
                if s <= dist:
                    recv(NB.at[piece(way, s), k], ay, (k, way, s - 1))
                    if s < dist:
                        tok(k, way, s)

    select(0)
    forward(1)
    select(1)
    select(2)
    forward(2)
    select(3)
    select(4)
    expert(0, 3)
    forward(3)
    select(5)
    select(6)
    expert(3, 5)
    forward(4)
    select(7)
    expert(5, 8)

    def own_sum(n):
        j = piece(*order[n])
        for i in range(1, 4):
            recv(RB.at[n, i], zb, (n, i - 1))
        RB[n, 0] = OB[n, 0]
        tail = jnp.zeros((64, W), F32)
        for k in range(3):
            rows = RB[n, :, :, W * k : W * (k + 1)].reshape(64, W)
            PS[j, k] = dot(WT[n, 0, :, 0:64], rows)
            tail = tail + dot(WT[n, k + 1, :, 0:64], rows)
        PS[j, 3] = tail

    def take(k, way, s):
        b = YB.at[k, way, s - 1]
        recv(b, rs, (k, way, s - 1))
        return b[...].astype(F32)

    def reduce(k, way, s):
        dist = far[k][way]
        if s < dist:
            dest = (y + dist - s) % RY if way == 0 else (y - dist + s + RY) % RY
            val = PS[dest, k]
            if s > 0:
                val = val + take(k, way, s)
            SB[k, way, s] = val.astype(BF)
            send(
                SB.at[k, way, s], YB.at[k, way, s], rs, (k, way, s),
                dev(dy=1 if way == 0 else -1),
            )

    own_sum(7)
    for k in range(C):
        reduce(k, k % 2, 0)
    own_sum(6)
    for k in range(C):
        if k % 2 == 1:
            reduce(k, 0, 0)
    own_sum(5)
    for k in range(C):
        if k % 2 == 0:
            reduce(k, 1, 0)
    for s in range(1, 4):
        for n in ((4, 3), (2, 1), (0,))[s - 1]:
            own_sum(n)
        for k in range(C):
            for way in (k % 2, 1 - k % 2):
                reduce(k, way, s)
    for k in range(C):
        cols = slice(W * k, W * (k + 1))
        total = HB[:, cols] + PS[y, k]
        for way in (1 - k % 2, k % 2):
            total = total + take(k, way, far[k][way])
        out_ref[:, cols] = total.astype(BF)
    for cp in sent:
        cp.wait_send()


def per_device(
    x_resid, q_latent, q_rope, cache_latent, cache_rope, new_latent, new_rope, w_uv, w_out,
    norm_gain, router, expert_ids, w_gate, w_up, w_down,
):
    vmem = pl.BlockSpec(memory_space=pltpu.VMEM)
    anyspace = pl.BlockSpec(memory_space=pl.ANY)
    dma = pltpu.SemaphoreType.DMA
    att, out = pl.pallas_call(
        kernel,
        out_shape=(jax.ShapeDtypeStruct((64, 2048), BF), jax.ShapeDtypeStruct((64, 2048), BF)),
        in_specs=[vmem] * 12 + [anyspace] * 3,
        out_specs=(vmem, vmem),
        scratch_shapes=[
            pltpu.VMEM((8, 16, 2, 80, 128), BF),
            pltpu.VMEM((704, 2048), BF),
            pltpu.VMEM((704, 2048), BF),
            pltpu.VMEM((704, 2048), BF),
            pltpu.VMEM((128, 512), BF),
            pltpu.VMEM((128, 64), BF),
            pltpu.VMEM((512, 128), BF),
            pltpu.VMEM((512, 512), BF),
            pltpu.VMEM((64, 1024), BF),
            pltpu.VMEM((64, 2048), F32),
            pltpu.VMEM((RY, C, 64, W), BF),
            pltpu.VMEM((RY, 64, 128), BF),
            pltpu.VMEM((RY, 4, 64, 128), BF),
            pltpu.VMEM((RY, 64, W), BF),
            pltpu.VMEM((RY, 3, PAD, 1536), BF),
            pltpu.VMEM((RY, 4, PAD, 1536), BF),
            pltpu.VMEM((RY, 4, PAD, 1536), BF),
            pltpu.VMEM((RY, 4, PAD, 1536), BF),
            pltpu.VMEM((RY, C, 64, W), F32),
            pltpu.VMEM((C, 2, 4, 64, W), BF),
            pltpu.VMEM((C, 2, 4, 64, W), BF),
            dma((3,)),
            dma((2, 3)),
            dma((2, 1)),
            dma((2, 2, RY)),
            dma((2, 2, 2, 4)),
            dma((2, RY, 4)),
            dma((2, C, 2, 4)),
            dma((2, 2, 4)),
            dma((2, RY, 3)),
            dma((2, RY, 3)),
            dma((2, C, 2, 4)),
        ],
        compiler_params=pltpu.CompilerParams(
            collective_id=0, has_side_effects=True, vmem_limit_bytes=56 << 20
        ),
    )(
        x_resid[0],
        q_latent.reshape(512, 512),
        q_rope.reshape(512, 64),
        cache_latent[0],
        cache_rope[0],
        new_latent[0],
        new_rope[0],
        w_uv,
        w_out,
        norm_gain.reshape(1, 2048),
        router.T,
        jnp.transpose(expert_ids, (2, 0, 1)),
        w_gate[0].T,
        w_up[0].T,
        w_down[0],
    )
    return att[None], out[None]


def solution(mesh):
    seq = P(("fsdp", "ep"), None, None)
    placed = (
        seq,
        P(("fsdp", "ep"), None, None, None),
        P(("fsdp", "ep"), None, None, None),
        seq,
        seq,
        seq,
        seq,
        P("fsdp", None, None),
        P("fsdp", None),
        P(),
        P(),
        seq,
        P("ep", None, None),
        P("ep", None, None),
        P("ep", None, None),
    )
    return jax.shard_map(
        per_device, mesh=mesh, in_specs=placed, out_specs=(seq, seq), check_vma=False
    )
```

time: 160 us -> 137 us (0.86)
  local copies, waits for them, and re-layouts: 15.6 us -> 3.34 us
  Pallas kernels: 143 us -> 132 us
    unnamed x9 -> x2, local copies, waits for them, and re-layouts: 15.6 us -> 3.34 us
    pallas_call x1, Pallas kernels: 143 us -> 132 us  [per_device(): pl.pallas_call(kernel, out_shape=(jax.ShapeDtypeStruct((64, 2048), BF), j...]
where the time goes in v2:
time: 137 us; the launch traced here: 136 us
  Pallas kernels  132 us (96%)
  local copies, waits for them, and re-layouts  3.34 us (2%)
    pallas_call x1, Pallas kernels, per_device(): pl.pallas_call(kernel, out_shape=(jax.ShapeDtypeStruct((64, 2048), BF), j...  132 us
    unnamed x2, local copies, waits for them, and re-layouts  3.34 us

profile of v2, /device:TPU:6, one launch (start us, length us, event | category | flops | bytes accessed | tf_op | source)
XLA Modules:
  0.0 136.0 jit_solution(935383760500465780)
XLA Ops:
  0.6 132.0 %shard_map.158 = (bf16[64,2048]{1,0:T(8,128)(2,1)}, bf16[64,2048]{1,0:T(8,128)(2,1)}) custom-call(bf16[64,2048]{1,0:T(8,128)(2,1)} %bitcast.23, bf16[512,512]{1,0:T(8,128)(2,1)} %bitcast.22, bf16[512,64]{1,0:T(8,128)(2,1)} %bitcast.26, bf16[64,512]{1,0:T(8,128)(2,1)} %bitcast.28, bf16[64,64]{1,0:T(8,128)(2,1)} %bitcast.30, bf16[64,512]{1,0:T(8,128)(2,1)} %bitcast.29, ...), custom_call_target="tpu_custom_call" | custom-call | tf_op jit(solution)/shard_map/pallas_call | solution.py:404
  132.6 1.7 %copy.19 = bf16[1,64,2048]{2,1,0:T(8,128)(2,1)} copy(bf16[1,64,2048]{2,1,0:T(8,128)(2,1)} %bitcast.25) | data formatting | bytes 524288
  134.3 1.7 %copy.20 = bf16[1,64,2048]{2,1,0:T(8,128)(2,1)} copy(bf16[1,64,2048]{2,1,0:T(8,128)(2,1)} %bitcast.24) | data formatting | bytes 524288

commit v3 on v2

--- a/solution.py
+++ b/solution.py
@@ -84,6 +84,9 @@
     pl.semaphore_wait(barrier, len(partners))
 
     own = G.at[y, mine, c]
+    x2 = (x + 2) % 4
+    facing = G.at[y, x2 * 4 + zh, c]
+    send(own, own, gx2, (0,), dev(dx=2))
     for d in range(1, 4):
         send(own, own, gz, (d - 1,), dev(dz=4 * d))
 
@@ -109,7 +112,9 @@
     for n in range(2):
         attend(n)
 
-    x2 = (x + 2) % 4
+    recv(facing, gx2, (0,))
+    for d in range(1, 4):
+        send(facing, facing, gz, (2 + d,), dev(dz=4 * d))
 
     def unit(j, xx, cx):
         return G.at[j, pl.ds(4 * xx, 4), cx]
@@ -136,18 +141,17 @@
     steps = [[4, 3], [3, 4]]
     for d in range(1, 4):
         recv(own, gz, (d - 1,))
-    u0 = unit(y, x, c)
-    send(u0, u0, gx2, (0,), dev(dx=2))
     for way in range(2):
         ring(y, x, 0, way, 0)
-    for n in range(2, 4):
-        attend(n)
-    recv(unit(y, x2, c), gx2, (0,))
+    attend(2)
+    for d in range(1, 4):
+        recv(facing, gz, (2 + d,))
     for way in range(2):
         ring(y, x2, 1, way, 0)
     to_x(y, 0)
     to_core(y, x, 0, 0)
     to_core(y, x2, 0, 1)
+    attend(3)
 
     def took_x(j, s):
         for i, xx in ((0, (x + 3) % 4), (1, (x + 1) % 4)):
@@ -239,28 +243,29 @@
     offs = [0, 1, -1, two]
     order = [(0, 0), (0, 1), (1, 1), (0, 2), (1, 2), (0, 3), (1, 3), (0, 4)]
 
+    lane = iota((128, 128), 1)
+    src = iota((128, 128), 0)
+    block = (lane >> 4) & 3
+    step = jnp.where(block == 1, 1, jnp.where(block == 2, -1, jnp.where(block == 3, two, 0)))
+    wanted = 4 * y + ((zl + step + 4) & 3)
+    pick_rank = jnp.where(src == wanted, 1.0, 0.0).astype(BF)
+    pick_gate = jnp.where(src == wanted + 32, 1.0, 0.0).astype(BF)
+    lane = iota((64, 128), 1)
+    low = lane & 15
+    places = [jnp.where(low < 12, low, -9)]
+    for q in range(3):
+        places.append(jnp.where(low >= 12, low - 12 + 4 * q, -9))
+    places = [p.astype(F32) for p in places]
+
     def select(n):
         j = piece(*order[n])
-        lane = iota((64, 128), 1)
-        m = MB[j].astype(F32)
-        hot = [jnp.zeros((64, 128), F32)] * 4
-        weight = [jnp.zeros((64, 128), F32)] * 4
-        for i in range(4):
-            e = 4 * y + (zl + offs[i] + 4) % 4
-            a = jnp.sum(jnp.where(lane == e, m, 0.0), axis=1, keepdims=True)
-            g = jnp.sum(jnp.where(lane == e + 32, m, 0.0), axis=1, keepdims=True)
-            for v in range(4):
-                if v == 0:
-                    hit = (a > -0.5) & (lane.astype(F32) == a + float(PAD * i))
-                else:
-                    d = a - float(4 * (v - 1))
-                    hit = (d > -0.5) & (d < 3.5) & (lane.astype(F32) == d + float(PAD * i + 12))
-                hot[v] = jnp.where(hit, 1.0, hot[v])
-                weight[v] = jnp.where(hit, g, weight[v])
+        m = MB[j]
+        ranks, gates = dot(m, pick_rank), dot(m, pick_gate)
         sel = []
         for v in range(4):
-            WT[n, v] = weight[v].astype(BF)
-            sel.append(hot[v].T.astype(BF)[0:64])
+            hit = ranks == places[v]
+            WT[n, v] = jnp.where(hit, gates, 0.0).astype(BF)
+            sel.append(jnp.where(hit, 1.0, 0.0).T.astype(BF)[0:64])
         last = NB[j, 3]
         for k in range(3):
             cols = slice(W * k, W * (k + 1))
@@ -328,13 +333,13 @@
     forward(2)
     select(3)
     select(4)
-    expert(0, 3)
     forward(3)
     select(5)
     select(6)
-    expert(3, 5)
+    expert(0, 3)
     forward(4)
     select(7)
+    expert(3, 5)
     expert(5, 8)
 
     def own_sum(n):
@@ -392,6 +397,11 @@
         out_ref[:, cols] = total.astype(BF)
     for cp in sent:
         cp.wait_send()
+
+
+def hand_on(att_in, out_in, att_ref, out_ref):
+    att_ref[...] = att_in[...]
+    out_ref[...] = out_in[...]
 
 
 def per_device(
@@ -429,7 +439,7 @@
             pltpu.VMEM((C, 2, 4, 64, W), BF),
             pltpu.VMEM((C, 2, 4, 64, W), BF),
             dma((3,)),
-            dma((2, 3)),
+            dma((2, 6)),
             dma((2, 1)),
             dma((2, 2, RY)),
             dma((2, 2, 2, 4)),
@@ -460,6 +470,12 @@
         w_up[0].T,
         w_down[0],
     )
+    att, out = pl.pallas_call(
+        hand_on,
+        out_shape=(jax.ShapeDtypeStruct((64, 2048), BF), jax.ShapeDtypeStruct((64, 2048), BF)),
+        in_specs=[vmem] * 2,
+        out_specs=(vmem, vmem),
+    )(att, out)
     return att[None], out[None]
 
 

time: 137 us -> 134 us (0.978)
  the two profiles are of different devices: /device:TPU:6 before, /device:TPU:8 now
where the time goes in v3:
time: 134 us; the launch traced here: 133 us
  Pallas kernels  133 us (99%)
    pallas_call x1, Pallas kernels, per_device(): pl.pallas_call(kernel, out_shape=(jax.ShapeDtypeStruct((64, 2048), BF), j...  131 us

profile of v3, /device:TPU:8, one launch (start us, length us, event | category | flops | bytes accessed | tf_op | source)
XLA Modules:
  0.0 133.5 jit_solution(8903216955720516082)
XLA Ops:
  0.6 131.0 %shard_map.158 = (bf16[64,2048]{1,0:T(8,128)(2,1)}, bf16[64,2048]{1,0:T(8,128)(2,1)}) custom-call(bf16[64,2048]{1,0:T(8,128)(2,1)} %bitcast.23, bf16[512,512]{1,0:T(8,128)(2,1)} %bitcast.22, bf16[512,64]{1,0:T(8,128)(2,1)} %bitcast.24, bf16[64,512]{1,0:T(8,128)(2,1)} %bitcast.26, bf16[64,64]{1,0:T(8,128)(2,1)} %bitcast.28, bf16[64,512]{1,0:T(8,128)(2,1)} %bitcast.27, ...), custom_call_target="tpu_custom_call" | custom-call | tf_op jit(solution)/shard_map/pallas_call | solution.py:414
  131.6 1.8 %shard_map.159 = (bf16[64,2048]{1,0:T(8,128)(2,1)}, bf16[64,2048]{1,0:T(8,128)(2,1)}) custom-call(bf16[64,2048]{1,0:T(8,128)(2,1)} %get-tuple-element.6.att_in, bf16[64,2048]{1,0:T(8,128)(2,1)} %get-tuple-element.7.out_in), custom_call_target="tpu_custom_call" | custom-call | tf_op jit(solution)/shard_map/pallas_call | solution.py:473
